TPU v7x, 32 devices: a whole 2x2x4 slice. The times are simulated.
32 devices in a mesh: row: 4 (over y, core), col: 8 (over z, x).
Axes of the slice: x: 2, y: 2, z: 4, core: 2. Of those that a mesh axis runs over, the one named last changes fastest.
Arguments:
- tensor: float32 [32, 1024, 2048], P(None, 'row', 'col'), may hold values from -120 to 120
- factor_b: float32 [2048, 256], P('col', 'row'), may hold values from -1 to 1
- factor_c: float32 [32, 256], replicated, may hold values from -5 to 5
Outputs:
- factor_a: float32 [1024, 256], P(('row', 'col'))
- col_scale: float32 [256], replicated
All inputs are finite; a program needn't handle non-finite values.
Results may differ from a plain program's by a relative error of at most 0.0003.
Values sent between devices are 32-bit elements; how exact they have to be, the bound alone decides.
A program may use at most 64 MiB of HBM per device.

v0:
```python
import jax
import jax.numpy as jnp
from jax import lax
from jax.sharding import PartitionSpec as P

eps = 1e-06


def contract_rows(slab, block_b, factor_c, high):
    depth, count, cols_j = slab.shape
    product = jnp.dot(
        slab.reshape(depth * count, cols_j),
        block_b,
        precision=high,
        preferred_element_type=jnp.float32,
    )
    product = product.reshape(depth, count, block_b.shape[1])
    return jnp.sum(product * factor_c[:, None, :], axis=0)


def sum_gram(partial_gram):
    return lax.psum(partial_gram, "col")


def local(tensor, factor_b, factor_c):
    high = lax.Precision.HIGHEST
    depth, rows_i, cols_j = tensor.shape
    block_b = lax.all_gather(factor_b, "row", axis=1, tiled=True)
    partial_gram = jnp.dot(block_b.T, block_b, precision=high, preferred_element_type=jnp.float32)
    gram_c = jnp.dot(factor_c.T, factor_c, precision=high, preferred_element_type=jnp.float32)
    share = rows_i // lax.axis_size("col")
    local_terms = contract_rows(tensor, block_b, factor_c, high)
    gram_b = sum_gram(partial_gram)
    summed = lax.psum(local_terms, "col")
    mine = lax.dynamic_slice_in_dim(summed, lax.axis_index("col") * share, share, 0)
    gram = gram_b * gram_c
    lower = jnp.linalg.cholesky(gram)
    half = lax.linalg.triangular_solve(lower, mine, left_side=False, lower=True, transpose_a=True)
    solved = lax.linalg.triangular_solve(
        lower, half, left_side=False, lower=True, transpose_a=False
    )
    squares = lax.psum(jnp.sum(solved * solved, axis=0), ("row", "col"))
    col_scale = jnp.sqrt(squares / (rows_i * lax.axis_size("row")) + eps)
    return (solved / col_scale, col_scale)


def solution(mesh):
    return jax.shard_map(
        local,
        mesh=mesh,
        in_specs=(P(None, "row", "col"), P("col", "row"), P()),
        out_specs=(P(("row", "col"), None), P()),
        check_vma=False,
    )
```

profile of v0, /device:TPU:0, one launch (start us, length us, event | category | flops | bytes accessed | tf_op | source)
XLA Modules:
  0.0 211.0 jit_solution(17414473705099297736)
XLA Ops:
  7.2 0.0 copy-start
  7.2 0.0 all-reduce.4.cloned.1.call-start
  7.2 7.4 %all_gather.3 = f32[256,256]{0,1:T(8,128)S(1)} all-gather(f32[256,64]{0,1:T(8,128)} %param.4), channel_id=1, replica_groups=mesh['row'=4,'col'=8] {'row'}, dimensions={1}, use_global_device_ids=true | all-gather | bytes 327680 | tf_op jit(solution)/shard_map/all_gather | solution.py:28
  14.7 1.1 fusion.15
  15.8 10.1 %multiply_reduce_fusion = f32[256,256]{1,0:T(8,128)} fusion(f32[32,256]{1,0:T(8,128)} %param.5, f32[32,256,256]{2,1,0:T(8,128)} %param.3, f32[256,256]{0,1:T(8,128)S(1)} %all_gather.3), kind=kOutput, calls=%fused_computation.2 | convolution fusion | flops 6446579712 | bytes 8945664 | tf_op jit(solution)/shard_map/dot_general | solution.py:11
  25.8 0.0 all-reduce.4.cloned.1.call-update
  25.9 74.0 %all-reduce.4.cloned.1.call-done = (f32[256,256]{0,1:T(8,128)}, f32[256,256]{1,0:T(8,128)}) async-done(((f32[256,256]{0,1:T(8,128)}, f32[256,256]{1,0:T(8,128)}), (f32[256,256]{0,1:T(8,128)}, f32[256,256]{1,0:T(8,128)})) %all-reduce.4.cloned.1.call-update) | async-done | bytes 524304 | tf_op jit(solution)/shard_map/psum | solution.py:22
  99.8 0.0 copy-done
  99.8 1.4 convolution_multiply_fusion
  101.2 0.1 copy.7
  101.4 11.7 %cholesky.50 = f32[128,128]{1,0:T(8,128)S(1)} custom-call(f32[128,128]{1,0:T(8,128)S(1)} %cholesky.118), custom_call_target="Cholesky" | custom-call | tf_op jit(solution)/shard_map/jit(cholesky)/cholesky | solution.py:37
  113.2 9.8 %custom-call.16 = f32[1,128,128]{1,2,0:T(8,128)S(1)} custom-call(f32[1,128,128]{2,1,0:T(8,128)S(1)} %get-tuple-element.25), custom_call_target="InvertDiagBlocksLowerTriangular" | custom-call | tf_op jit(solution)/shard_map/jit(cholesky)/cholesky | solution.py:37
  123.0 0.2 constant_dynamic-update-slice_fusion.1
  123.2 0.3 convolution_subtract_fusion
  123.5 11.7 %cholesky.105 = f32[128,128]{1,0:T(8,128)S(1)} custom-call(f32[128,128]{1,0:T(8,128)S(1)} %convolution_subtract_fusion), custom_call_target="Cholesky" | custom-call | tf_op jit(solution)/shard_map/jit(cholesky)/cholesky | solution.py:37
  135.2 0.7 compare_reduce_fusion
  137.2 0.1 triangular_solve.67
  137.3 3.9 %while.1 = (s32[]{:T(128)}, f32[256,256]{1,0:T(8,128)S(1)}, s32[2,2]{1,0:T(2,128)S(1)}, f32[2,128,128]{2,1,0:T(8,128)S(1)}, s32[]{:T(128)}) while((s32[]{:T(128)}, f32[256,256]{1,0:T(8,128)S(1)}, s32[2,2]{1,0:T(2,128)S(1)}, f32[2,128,128]{2,1,0:T(8,128)S(1)}, s32[]{:T(128)}) %tuple.27), condition=%wide.while_cond, body=%wide.while_body.sunk | while | flops 2 | bytes 131181 | solution.py:38
  137.3 0.6 fusion.29
  137.9 1.4 bitcast_dynamic-update-slice_fusion.2
  139.3 0.6 fusion.29
  139.9 1.4 bitcast_dynamic-update-slice_fusion.2
  141.3 19.9 %custom-call.17 = f32[2,128,128]{1,2,0:T(8,128)S(1)} custom-call(f32[2,128,128]{2,1,0:T(8,128)S(1)} %get-tuple-element.9), custom_call_target="InvertDiagBlocksLowerTriangular" | custom-call | tf_op jit(solution)/shard_map/triangular_solve | solution.py:38
  161.2 0.9 fusion.6
  162.0 0.9 convolution_subtract_fusion.2
  163.0 0.2 fusion.8
  163.2 0.2 fusion.7
  163.4 0.2 convolution_subtract_fusion.1
  163.6 0.2 fusion.5
  163.8 39.7 %psum.23 = f32[256]{0:T(256)S(1)} all-reduce(f32[256]{0:T(256)S(1)} %multiply_reduce_fusion.1), channel_id=1, replica_groups=mesh['row'=4,'col'=8] {'row','col'}, use_global_device_ids=true, to_apply=%region_8.9 | all-reduce | flops 256 | bytes 2048 | tf_op jit(solution)/shard_map/psum | solution.py:42
  203.5 0.6 fusion.11
  204.1 0.0 copy-done.1
  (13 shorter events, 0.2 us)
Async XLA Ops:
  7.2 92.7 %copy-start = (f32[32,256]{1,0:T(8,128)S(1)}, f32[32,256]{1,0:T(8,128)}, u32[]{:S(2)}) copy-start(f32[32,256]{1,0:T(8,128)} %param.5) | copy-start | bytes 98308
  7.2 92.7 %all-reduce.4.cloned.1.call-start = ((), (), s32[]{:S(2)}) async-start(), calls=%async_computation | async-start | bytes 1048576 | tf_op jit(solution)/shard_map/psum | solution.py:22
  203.5 0.6 copy-start.1
Sparse Core Ops, SparseCore 0:
  26.0 73.8 all-reduce.3
where the time goes:
time: 211 us
  waiting for transfers between devices  74 us (35%)
  other arithmetic  54.7 us (26%)
  blocking collectives  47.1 us (22%)
  matrix products  15.5 us (7%)
  between operations  15.5 us (7%)
  local copies, waits for them, and re-layouts  4.14 us (2%)
    psum x1, waiting for transfers between devices, sum_gram(): return lax.psum(partial_gram, 'col')  74 us
    psum x1, blocking collectives, local(): squares = lax.psum(jnp.sum(solved * solved, axis=0), ('row', 'col'))  39.7 us
    another operation x6, other arithmetic, local(): lower = jnp.linalg.cholesky(gram)  34 us
    another operation x3, other arithmetic, local(): lax.linalg.triangular_solve(lower, mine, left_side=False, lower=True, tra...  19.9 us
    dot_general x1, matrix products, contract_rows(): jnp.dot(slab.reshape(depth * count, cols_j), block_b, precision=high, pre...  10.1 us
    all_gather x1, blocking collectives, local(): block_b = lax.all_gather(factor_b, 'row', axis=1, tiled=True)  7.43 us
  transfers between devices with their start and end apart: 1, of which 1 were waited for; matrix products, arithmetic and copies ran while one was open for 0% of the time, Pallas kernels for 0%

commit v1 on v0

v1 whole, which is shorter than its diff:
```python
import functools

import jax
import jax.numpy as jnp
from jax import lax
from jax.experimental import pallas as pl
from jax.experimental.pallas import tpu as pltpu
from jax.sharding import PartitionSpec as P

eps = 1e-06
MESH = pl.DeviceIdType.MESH
HIGH = lax.Precision.HIGHEST
TOP = 64
SUB = 8


def push(src, dst, ssem, rsem, device):
    return pltpu.make_async_remote_copy(
        src_ref=src, dst_ref=dst, send_sem=ssem, recv_sem=rsem,
        device_id=device, device_id_type=MESH,
    )


def greet(nr, nc):
    me_r, me_c = lax.axis_index("row"), lax.axis_index("col")
    barrier = pltpu.get_barrier_semaphore()
    for n in range(1, nr):
        pl.semaphore_signal(barrier, inc=1, device_id={"row": lax.rem(me_r + n, nr)}, device_id_type=MESH)
    for n in range(1, nc):
        pl.semaphore_signal(barrier, inc=1, device_id={"col": lax.rem(me_c + n, nc)}, device_id_type=MESH)
    pl.semaphore_wait(barrier, nr + nc - 2)


def nt_dot(a, b, precision=None):
    return lax.dot_general(
        a, b, (((1,), (1,)), ((), ())), precision=precision, preferred_element_type=jnp.float32
    )


def terms_kernel(
    nr, nc, t_ref, b_ref, c_ref, gram_ref, mine_ref,
    bt, bh, bl, gc, gsend, grecv, gfull, msend, mrecv, tbuf,
    tsem, bs, br, gs, gr_, cs, cr, rs, rr, ms, mr,
):
    me_r, me_c = lax.axis_index("row"), lax.axis_index("col")
    depth, share = tbuf.shape[1], tbuf.shape[2]
    rb = b_ref.shape[1]
    rows = gsend.shape[1]
    ranks = bt.shape[0]

    def load(n):
        p = lax.rem(me_c + n, nc)
        start = pl.multiple_of(p * share, share)
        return pltpu.make_async_copy(t_ref.at[:, pl.ds(start, share), :], tbuf.at[n], tsem.at[n])

    for n in list(range(1, nc)) + [0]:
        load(n).start()
    mine_rows = pl.ds(pl.multiple_of(me_r * rb, rb), rb)
    own = b_ref[...].T
    bt[mine_rows, :] = own
    greet(nr, nc)

    copies = []
    for n in range(1, nr):
        copies.append(push(bt.at[mine_rows], bt.at[mine_rows], bs.at[n], br.at[n], {"row": lax.rem(me_r + n, nr)}))
        copies[-1].start()
    c = c_ref[...]
    gc[...] = lax.dot_general(
        c, c, (((0,), (0,)), ((), ())), precision=HIGH, preferred_element_type=jnp.float32
    )
    for n in range(1, nr):
        came = pl.ds(pl.multiple_of(lax.rem(me_r + nr - n, nr) * rb, rb), rb)
        push(bt.at[mine_rows], bt.at[came], bs.at[n], br.at[n], {"row": lax.rem(me_r + n, nr)}).wait_recv()

    full = bt[...]
    part = nt_dot(own, full, HIGH)
    for n in range(nc):
        gsend[n] = part[n * rows:(n + 1) * rows]
    gcopies = []
    for n in range(1, nc):
        p = lax.rem(me_c + n, nc)
        gcopies.append(push(gsend.at[p], grecv.at[n], gs.at[n], gr_.at[n], {"col": p}))
        gcopies[-1].start()
    hi = full.astype(jnp.bfloat16)
    bh[...] = hi
    bl[...] = (full - hi.astype(jnp.float32)).astype(jnp.bfloat16)

    group = max(1, 512 // share)

    def block(n):
        load(n).wait()
        total = jnp.zeros((share, ranks), jnp.float32)
        for g in range(0, depth, group):
            slab = tbuf[n, g:g + group].reshape(group * share, tbuf.shape[3])
            th = slab.astype(jnp.bfloat16)
            tl = (slab - th.astype(jnp.float32)).astype(jnp.bfloat16)
            product = nt_dot(th, bh[...]) + (nt_dot(tl, bh[...]) + nt_dot(th, bl[...]))
            for f in range(group):
                total += product[f * share:(f + 1) * share] * c_ref[g + f:g + f + 1, :]
        msend[n] = total

    def block_send(n):
        return push(msend.at[n], mrecv.at[n], ms.at[n], mr.at[n], {"col": lax.rem(me_c + n, nc)})

    def blocks(first, last):
        @pl.loop(first, last)
        def _(n):
            block(n)
            block_send(n).start()

    cut1, cut2 = nc // 4 + 1, nc // 2 + 1
    blocks(1, cut1)
    for copy in gcopies:
        copy.wait_recv()
    total = gsend[me_c]
    for n in range(1, nc):
        total = total + grecv[n]
    gfull[me_r, me_c] = total
    ccopies = []
    for n in range(1, nc):
        slot = gfull.at[me_r, me_c]
        ccopies.append(push(slot, slot, cs.at[n], cr.at[n], {"col": lax.rem(me_c + n, nc)}))
        ccopies[-1].start()
    blocks(cut1, cut2)
    for n in range(1, nc):
        came = gfull.at[me_r, lax.rem(me_c + nc - n, nc)]
        push(gfull.at[me_r, me_c], came, cs.at[n], cr.at[n], {"col": lax.rem(me_c + n, nc)}).wait_recv()
    rcopies = []
    for n in range(1, nr):
        slot = gfull.at[me_r]
        rcopies.append(push(slot, slot, rs.at[n], rr.at[n], {"row": lax.rem(me_r + n, nr)}))
        rcopies[-1].start()
    blocks(cut2, nc)
    block(0)
    for n in range(1, nr):
        came = gfull.at[lax.rem(me_r + nr - n, nr)]
        push(gfull.at[me_r], came, rs.at[n], rr.at[n], {"row": lax.rem(me_r + n, nr)}).wait_recv()
    for r in range(nr):
        for k in range(nc):
            at = (r * nc + k) * rows
            gram_ref[r, k] = gfull[r, k] * gc[at:at + rows, :]
    total = msend[0]
    for n in range(1, nc):
        block_send(n).wait_recv()
        total = total + mrecv[n]
    mine_ref[...] = total
    for copy in copies + gcopies + ccopies + rcopies:
        copy.wait_send()
    for n in range(1, nc):
        block_send(n).wait_send()


def invert_block(tile, low):
    size = TOP // SUB
    lane = lax.broadcasted_iota(jnp.int32, (SUB, 2 * TOP), 1)
    row = lax.broadcasted_iota(jnp.int32, (SUB, 2 * TOP), 0)
    held = (lane < TOP) if low else (lane >= TOP)
    shift = TOP if low else 0
    base = 0 if low else TOP
    v = []
    for i in range(size):
        unit = (lane == row + (shift + i * SUB)).astype(jnp.float32)
        v.append(jnp.where(held, tile[i * SUB:(i + 1) * SUB], unit))
    wide = (SUB, 2 * TOP)
    for s in range(size):
        cols = [
            [jnp.broadcast_to(v[i][:, base + s * SUB + j:base + s * SUB + j + 1], wide) for j in range(SUB)]
            for i in range(size)
        ]
        head, c = v[s], cols[s]
        for p in range(SUB):
            inv = 1.0 / jnp.broadcast_to(c[p][p:p + 1], wide)
            here = row == p
            pivot = jnp.broadcast_to(head[p:p + 1], wide) * inv
            head = jnp.where(here, pivot, head - c[p] * pivot)
            for j in range(p + 1, SUB):
                q = jnp.broadcast_to(c[j][p:p + 1], wide) * inv
                c[j] = jnp.where(here, q, c[j] - c[p] * q)
        lines = [jnp.broadcast_to(head[j:j + 1], wide) for j in range(SUB)]
        for i in range(size):
            if i == s:
                v[i] = head
            else:
                terms = [cols[i][j] * lines[j] for j in range(SUB)]
                while len(terms) > 1:
                    terms = [a + b for a, b in zip(terms[::2], terms[1::2])]
                v[i] = v[i] - terms[0]
    whole = jnp.concatenate(v, axis=0)
    return whole[:, shift:shift + TOP]


def solve_kernel(gram_ref, mine_ref, solved_ref, squares_ref, a):
    ranks = gram_ref.shape[0]
    share = mine_ref.shape[0]
    a[0:ranks, :] = gram_ref[...]
    a[ranks:, :] = mine_ref[...]
    for b in range(ranks // TOP):
        at = b * TOP
        inverse = invert_block(a[at:at + TOP, (b // 2) * 2 * TOP:(b // 2 + 1) * 2 * TOP], b % 2 == 0)
        below = a[at + TOP:, :]
        w = jnp.dot(below[:, at:at + TOP], inverse, precision=HIGH, preferred_element_type=jnp.float32)
        change = jnp.dot(w, a[at:at + TOP, :], precision=HIGH, preferred_element_type=jnp.float32)
        a[at + TOP:, :] = below - change
        a[at + TOP:, at:at + TOP] = w
    solved = a[ranks:, :]
    solved_ref[...] = solved
    squares_ref[...] = jnp.sum(solved * solved, axis=0, keepdims=True)


def scale_kernel(nr, nc, count, solved_ref, squares_ref, out_ref, scale_ref, first, second, cs, cr, rs, rr):
    me_r, me_c = lax.axis_index("row"), lax.axis_index("col")
    first[me_c] = squares_ref[...]
    greet(nr, nc)
    for buf, me, n_all, ss, sr, name in (
        (first, me_c, nc, cs, cr, "col"), (second, me_r, nr, rs, rr, "row")
    ):
        if name == "row":
            total = first[0]
            for n in range(1, nc):
                total = total + first[n]
            second[me_r] = total
        slot = buf.at[me]
        copies = [
            push(slot, slot, ss.at[n], sr.at[n], {name: lax.rem(me + n, n_all)}) for n in range(1, n_all)
        ]
        for copy in copies:
            copy.start()
        for n in range(1, n_all):
            came = buf.at[lax.rem(me + n_all - n, n_all)]
            push(slot, came, ss.at[n], sr.at[n], {name: lax.rem(me + n, n_all)}).wait_recv()
        for copy in copies:
            copy.wait_send()
    total = second[0]
    for n in range(1, nr):
        total = total + second[n]
    scale = jnp.sqrt(total / count + eps)
    scale_ref[...] = scale
    out_ref[...] = solved_ref[...] / scale


def local(tensor, factor_b, factor_c):
    depth, rows_i, cols_j = tensor.shape
    ranks = factor_c.shape[1]
    rb = factor_b.shape[1]
    nr, nc = lax.axis_size("row"), lax.axis_size("col")
    share = rows_i // nc
    rows = ranks // (nr * nc)
    f32, bf16 = jnp.float32, jnp.bfloat16
    vmem = pl.BlockSpec(memory_space=pltpu.VMEM)
    dma = pltpu.SemaphoreType.DMA
    gram, mine = pl.pallas_call(
        functools.partial(terms_kernel, nr, nc),
        out_shape=(
            jax.ShapeDtypeStruct((nr, nc, rows, ranks), f32),
            jax.ShapeDtypeStruct((share, ranks), f32),
        ),
        in_specs=[pl.BlockSpec(memory_space=pl.ANY), vmem, vmem],
        out_specs=(vmem, vmem),
        scratch_shapes=[
            pltpu.VMEM((ranks, cols_j), f32),
            pltpu.VMEM((ranks, cols_j), bf16),
            pltpu.VMEM((ranks, cols_j), bf16),
            pltpu.VMEM((ranks, ranks), f32),
            pltpu.VMEM((nc, rows, ranks), f32),
            pltpu.VMEM((nc, rows, ranks), f32),
            pltpu.VMEM((nr, nc, rows, ranks), f32),
            pltpu.VMEM((nc, share, ranks), f32),
            pltpu.VMEM((nc, share, ranks), f32),
            pltpu.VMEM((nc, depth, share, cols_j), f32),
            dma((nc,)), dma((nr,)), dma((nr,)), dma((nc,)), dma((nc,)), dma((nc,)), dma((nc,)),
            dma((nr,)), dma((nr,)), dma((nc,)), dma((nc,)),
        ],
        compiler_params=pltpu.CompilerParams(
            collective_id=0, has_side_effects=True, vmem_limit_bytes=40 * 2**20
        ),
        name="terms",
    )(tensor, factor_b, factor_c)
    solved, squares = pl.pallas_call(
        solve_kernel,
        out_shape=(jax.ShapeDtypeStruct((share, ranks), f32), jax.ShapeDtypeStruct((1, ranks), f32)),
        in_specs=[vmem, vmem],
        out_specs=(vmem, vmem),
        scratch_shapes=[pltpu.VMEM((ranks + share, ranks), f32)],
        compiler_params=pltpu.CompilerParams(vmem_limit_bytes=32 * 2**20),
        name="solve",
    )(gram.reshape(ranks, ranks), mine)
    factor_a, col_scale = pl.pallas_call(
        functools.partial(scale_kernel, nr, nc, float(rows_i * nr)),
        out_shape=(jax.ShapeDtypeStruct((share, ranks), f32), jax.ShapeDtypeStruct((1, ranks), f32)),
        in_specs=[vmem, vmem],
        out_specs=(vmem, vmem),
        scratch_shapes=[
            pltpu.VMEM((nc, 1, ranks), f32), pltpu.VMEM((nr, 1, ranks), f32),
            dma((nc,)), dma((nc,)), dma((nr,)), dma((nr,)),
        ],
        compiler_params=pltpu.CompilerParams(collective_id=1, has_side_effects=True),
        name="scale",
    )(solved, squares)
    return (factor_a, col_scale.reshape(ranks))


def solution(mesh):
    return jax.shard_map(
        local,
        mesh=mesh,
        in_specs=(P(None, "row", "col"), P("col", "row"), P()),
        out_specs=(P(("row", "col"), None), P()),
        check_vma=False,
    )
```

time: 211 us -> 58 us (0.27)
  waiting for transfers between devices: 74 us -> 0 us
  other arithmetic: 54.7 us -> 0 us
  Pallas kernels: 0 us -> 48.1 us
  blocking collectives: 47.1 us -> 0 us
  matrix products: 15.5 us -> 0 us
  between operations: 15.5 us -> 0.67 us
  local copies, waits for them, and re-layouts: 4.14 us -> 8.84 us
    psum x1 -> x0, waiting for transfers between devices: 74 us -> none  [sum_gram(): return lax.psum(partial_gram, 'col')]
    another operation x9 -> x0, other arithmetic: 53.9 us -> none  [the longest x6 34 us: local(): lower = jnp.linalg.cholesky(gram)]
    pallas_call x0 -> x3, Pallas kernels: none -> 48.1 us  [the longest x1 25.7 us: local(): pl.pallas_call(functools.partial(terms_kernel, nr, nc), out_shape=(jax.Sh...]
    psum x1 -> x0, blocking collectives: 39.7 us -> none  [local(): squares = lax.psum(jnp.sum(solved * solved, axis=0), ('row', 'col'))]
    dot_general x3 -> x0, matrix products: 12.5 us -> none  [the longest x1 10.1 us: contract_rows(): jnp.dot(slab.reshape(depth * count, cols_j), block_b, precision=high, pre...]
    unnamed x4 -> x11, local copies, waits for them, and re-layouts: 0.01 us -> 8.84 us
    all_gather x1 -> x0, blocking collectives: 7.43 us -> none  [local(): block_b = lax.all_gather(factor_b, 'row', axis=1, tiled=True)]
    another operation x9 -> x0, local copies, waits for them, and re-layouts: 4 us -> none
  transfers between devices with their start and end apart: 1 -> 0, of which waited for: 1 -> 0; matrix products, arithmetic and copies ran while one was open for 0% -> 0% of each run, Pallas kernels for 0% -> 0%
where the time goes in v1:
time: 58 us; the launch traced here: 57.6 us
  Pallas kernels  48.1 us (83%)
  local copies, waits for them, and re-layouts  8.84 us (15%)
  between operations  0.67 us (1%)
    pallas_call x1, Pallas kernels, local(): pl.pallas_call(functools.partial(terms_kernel, nr, nc), out_shape=(jax.Sh...  25.7 us
    pallas_call x1, Pallas kernels, local(): pl.pallas_call(solve_kernel, out_shape=(jax.ShapeDtypeStruct((share, rank...  11.6 us
    pallas_call x1, Pallas kernels, local(): pl.pallas_call(functools.partial(scale_kernel, nr, nc, float(rows_i * nr)...  10.7 us
    unnamed x11, local copies, waits for them, and re-layouts  8.84 us

profile of v1, /device:TPU:0, one launch (start us, length us, event | category | flops | bytes accessed | tf_op | source)
XLA Modules:
  0.0 57.6 jit_solution(2009338808509512584)
XLA Ops:
  0.6 0.9 %copy.5.b_ref = f32[256,64]{1,0:T(8,128)S(1)} copy(f32[256,64]{0,1:T(8,128)} %param.4) | data formatting | bytes 131072 | tf_op args[1]
  1.6 0.0 copy-start
  1.6 3.4 %copy-done = f32[32,256,256]{2,1,0:T(8,128)S(1)} copy-done((f32[32,256,256]{2,1,0:T(8,128)S(1)}, f32[32,256,256]{2,1,0:T(8,128)}, u32[]{:S(2)}) %copy-start) | copy-done | bytes 8388632
  5.0 0.0 copy-start.1
  5.0 0.8 %copy-done.1 = f32[32,256]{1,0:T(8,128)S(1)} copy-done((f32[32,256]{1,0:T(8,128)S(1)}, f32[32,256]{1,0:T(8,128)}, u32[]{:S(2)}) %copy-start.1) | copy-done | bytes 32792
  5.7 25.7 %terms.1 = (f32[4,8,8,256]{3,2,1,0:T(8,128)S(1)}, f32[32,256]{1,0:T(8,128)S(1)}) custom-call(f32[32,256,256]{2,1,0:T(8,128)S(1)} %copy-done, f32[256,64]{1,0:T(8,128)S(1)} %copy.5.b_ref, f32[32,256]{1,0:T(8,128)S(1)} %copy-done.1), custom_call_target="tpu_custom_call" | custom-call | tf_op jit(solution)/shard_map/terms/pallas_call | solution.py:251
  31.4 11.6 %solve.1 = (f32[32,256]{1,0:T(8,128)S(1)}, f32[1,256]{1,0:T(1,128)S(1)}) custom-call(f32[256,256]{1,0:T(8,128)S(1)} %bitcast.2, f32[32,256]{1,0:T(8,128)S(1)} %get-tuple-element.9.mine_ref), custom_call_target="tpu_custom_call" | custom-call | tf_op jit(solution)/shard_map/solve/pallas_call | solution.py:278
  43.1 0.0 copy-start.2
  43.1 0.6 %copy-done.2 = f32[32,256]{1,0:T(8,128)} copy-done((f32[32,256]{1,0:T(8,128)}, f32[32,256]{1,0:T(8,128)S(1)}, u32[]{:S(2)}) %copy-start.2) | copy-done | bytes 32792
  43.7 0.0 copy-start.3
  43.7 0.6 copy-done.3
  44.3 10.7 %scale.1 = (f32[32,256]{1,0:T(8,128)}, f32[1,256]{1,0:T(1,128)}) custom-call(f32[32,256]{1,0:T(8,128)} %copy-done.2, f32[1,256]{1,0:T(1,128)} %copy-done.3), custom_call_target="tpu_custom_call" | custom-call | tf_op jit(solution)/shard_map/scale/pallas_call | solution.py:287
  55.0 1.4 %copy.8 = f32[32,256]{1,0:T(8,128)} copy(f32[32,256]{1,0:T(8,128)} %get-tuple-element.16) | data formatting | bytes 65536
  56.4 1.2 %copy.9 = f32[256]{0:T(256)} copy(f32[256]{0:T(256)} %bitcast.3) | data formatting | bytes 2048
Async XLA Ops:
  1.6 3.4 %copy-start = (f32[32,256,256]{2,1,0:T(8,128)S(1)}, f32[32,256,256]{2,1,0:T(8,128)}, u32[]{:S(2)}) copy-start(f32[32,256,256]{2,1,0:T(8,128)} %t_ref.1) | copy-start | bytes 25165828
  5.0 0.8 %copy-start.1 = (f32[32,256]{1,0:T(8,128)S(1)}, f32[32,256]{1,0:T(8,128)}, u32[]{:S(2)}) copy-start(f32[32,256]{1,0:T(8,128)} %c_ref.1) | copy-start | bytes 98308
  43.1 0.6 %copy-start.2 = (f32[32,256]{1,0:T(8,128)}, f32[32,256]{1,0:T(8,128)S(1)}, u32[]{:S(2)}) copy-start(f32[32,256]{1,0:T(8,128)S(1)} %get-tuple-element.10.solved_ref) | copy-start | bytes 98308
  43.7 0.6 copy-start.3

commit v2 on v1

v2 whole, which is shorter than its diff:
```python
import functools

import jax
import jax.numpy as jnp
from jax import lax
from jax.experimental import pallas as pl
from jax.experimental.pallas import tpu as pltpu
from jax.sharding import PartitionSpec as P

eps = 1e-06
MESH = pl.DeviceIdType.MESH
HIGH = lax.Precision.HIGHEST
TOP = 64
SUB = 8


def push(src, dst, ssem, rsem, device):
    return pltpu.make_async_remote_copy(
        src_ref=src, dst_ref=dst, send_sem=ssem, recv_sem=rsem,
        device_id=device, device_id_type=MESH,
    )


def greet(nr, nc):
    me_r, me_c = lax.axis_index("row"), lax.axis_index("col")
    barrier = pltpu.get_barrier_semaphore()
    for n in range(1, nr):
        pl.semaphore_signal(barrier, inc=1, device_id={"row": lax.rem(me_r + n, nr)}, device_id_type=MESH)
    for n in range(1, nc):
        pl.semaphore_signal(barrier, inc=1, device_id={"col": lax.rem(me_c + n, nc)}, device_id_type=MESH)
    return lambda: pl.semaphore_wait(barrier, nr + nc - 2)


def nt_dot(a, b, precision=None):
    return lax.dot_general(
        a, b, (((1,), (1,)), ((), ())), precision=precision, preferred_element_type=jnp.float32
    )


def invert_block(tile, low):
    size = TOP // SUB
    lane = lax.broadcasted_iota(jnp.int32, (SUB, 2 * TOP), 1)
    row = lax.broadcasted_iota(jnp.int32, (SUB, 2 * TOP), 0)
    held = (lane < TOP) if low else (lane >= TOP)
    shift = TOP if low else 0
    base = 0 if low else TOP
    v = []
    for i in range(size):
        unit = (lane == row + (shift + i * SUB)).astype(jnp.float32)
        v.append(jnp.where(held, tile[i * SUB:(i + 1) * SUB], unit))
    wide = (SUB, 2 * TOP)
    for s in range(size):
        cols = [
            [jnp.broadcast_to(v[i][:, base + s * SUB + j:base + s * SUB + j + 1], wide) for j in range(SUB)]
            for i in range(size)
        ]
        head, c = v[s], cols[s]
        for p in range(SUB):
            inv = 1.0 / jnp.broadcast_to(c[p][p:p + 1], wide)
            here = row == p
            pivot = jnp.broadcast_to(head[p:p + 1], wide) * inv
            head = jnp.where(here, pivot, head - c[p] * pivot)
            for j in range(p + 1, SUB):
                q = jnp.broadcast_to(c[j][p:p + 1], wide) * inv
                c[j] = jnp.where(here, q, c[j] - c[p] * q)
        lines = [jnp.broadcast_to(head[j:j + 1], wide) for j in range(SUB)]
        for i in range(size):
            if i == s:
                v[i] = head
            else:
                terms = [cols[i][j] * lines[j] for j in range(SUB)]
                while len(terms) > 1:
                    terms = [a + b for a, b in zip(terms[::2], terms[1::2])]
                v[i] = v[i] - terms[0]
    whole = jnp.concatenate(v, axis=0)
    return whole[:, shift:shift + TOP]


def whole_kernel(
    nr, nc, t_ref, b_hbm, c_hbm, solved_ref, squares_ref,
    bt, bcat, gc, gsend, grecv, gfull, msend, mrecv, tbuf, c_ref, a, first, second,
    tsem, lsem, bs, br, gs, gr_, cs, cr, rs, rr, ms, mr, qs, qr, us, ur,
):
    me_r, me_c = lax.axis_index("row"), lax.axis_index("col")
    depth, share = tbuf.shape[1], tbuf.shape[2]
    rb = b_hbm.shape[0]
    rows = gsend.shape[1]
    ranks = bt.shape[0]

    def load(n):
        p = lax.rem(me_c + n, nc)
        start = pl.multiple_of(p * share, share)
        return pltpu.make_async_copy(t_ref.at[:, pl.ds(start, share), :], tbuf.at[n], tsem.at[n])

    greeted = greet(nr, nc)
    mine_rows = pl.ds(pl.multiple_of(me_r * rb, rb), rb)
    own_copy = pltpu.make_async_copy(b_hbm, bt.at[mine_rows], lsem.at[0])
    c_copy = pltpu.make_async_copy(c_hbm, c_ref, lsem.at[1])
    own_copy.start()
    c_copy.start()
    for n in list(range(1, nc)) + [0]:
        load(n).start()
    greeted()

    copies = []
    for n in range(1, nr):
        copies.append(push(b_hbm, bt.at[mine_rows], bs.at[n], br.at[n], {"row": lax.rem(me_r + n, nr)}))
        copies[-1].start()
    c_copy.wait()
    c = c_ref[...]
    gc[...] = lax.dot_general(
        c, c, (((0,), (0,)), ((), ())), precision=HIGH, preferred_element_type=jnp.float32
    )
    for n in range(1, nr):
        came = pl.ds(pl.multiple_of(lax.rem(me_r + nr - n, nr) * rb, rb), rb)
        push(b_hbm, bt.at[came], bs.at[n], br.at[n], {"row": lax.rem(me_r + n, nr)}).wait_recv()

    own_copy.wait()
    full = bt[...]
    own = bt[mine_rows, :]
    part = nt_dot(own, full, HIGH)
    for n in range(nc):
        gsend[n] = part[n * rows:(n + 1) * rows]
    gcopies = []
    for n in range(1, nc):
        p = lax.rem(me_c + n, nc)
        gcopies.append(push(gsend.at[p], grecv.at[n], gs.at[n], gr_.at[n], {"col": p}))
        gcopies[-1].start()
    hi = full.astype(jnp.bfloat16)
    lo = (full - hi.astype(jnp.float32)).astype(jnp.bfloat16)
    bcat[...] = jnp.concatenate([hi, hi, lo], axis=1)

    group = max(1, 512 // share)

    def block(n):
        load(n).wait()
        total = jnp.zeros((share, ranks), jnp.float32)
        for g in range(0, depth, group):
            slab = tbuf[n, g:g + group].reshape(group * share, tbuf.shape[3])
            th = slab.astype(jnp.bfloat16)
            tl = (slab - th.astype(jnp.float32)).astype(jnp.bfloat16)
            product = nt_dot(jnp.concatenate([th, tl, th], axis=1), bcat[...])
            for f in range(group):
                total += product[f * share:(f + 1) * share] * c_ref[g + f:g + f + 1, :]
        msend[n] = total

    def block_send(n):
        return push(msend.at[n], mrecv.at[n], ms.at[n], mr.at[n], {"col": lax.rem(me_c + n, nc)})

    def blocks(first, last):
        @pl.loop(first, last)
        def _(n):
            block(n)
            block_send(n).start()

    cut1, cut2 = nc // 4 + 1, nc // 2 + 1
    blocks(1, cut1)
    for copy in gcopies:
        copy.wait_recv()
    total = gsend[me_c]
    for n in range(1, nc):
        total = total + grecv[n]
    gfull[me_r, me_c] = total
    ccopies = []
    for n in range(1, nc):
        slot = gfull.at[me_r, me_c]
        ccopies.append(push(slot, slot, cs.at[n], cr.at[n], {"col": lax.rem(me_c + n, nc)}))
        ccopies[-1].start()
    blocks(cut1, cut2)
    for n in range(1, nc):
        came = gfull.at[me_r, lax.rem(me_c + nc - n, nc)]
        push(gfull.at[me_r, me_c], came, cs.at[n], cr.at[n], {"col": lax.rem(me_c + n, nc)}).wait_recv()
    rcopies = []
    for n in range(1, nr):
        slot = gfull.at[me_r]
        rcopies.append(push(slot, slot, rs.at[n], rr.at[n], {"row": lax.rem(me_r + n, nr)}))
        rcopies[-1].start()
    blocks(cut2, nc)
    block(0)
    for n in range(1, nr):
        came = gfull.at[lax.rem(me_r + nr - n, nr)]
        push(gfull.at[me_r], came, rs.at[n], rr.at[n], {"row": lax.rem(me_r + n, nr)}).wait_recv()
    for r in range(nr):
        for k in range(nc):
            at = (r * nc + k) * rows
            a[at:at + rows, :] = gfull[r, k] * gc[at:at + rows, :]

    for b in range(ranks // TOP):
        at = b * TOP
        inverse = invert_block(a[at:at + TOP, (b // 2) * 2 * TOP:(b // 2 + 1) * 2 * TOP], b % 2 == 0)
        if b == 0:
            total = msend[0]
            for n in range(1, nc):
                block_send(n).wait_recv()
                total = total + mrecv[n]
            a[ranks:, :] = total
        below = a[at + TOP:, :]
        w = jnp.dot(below[:, at:at + TOP], inverse, precision=HIGH, preferred_element_type=jnp.float32)
        change = jnp.dot(w, a[at:at + TOP, :], precision=HIGH, preferred_element_type=jnp.float32)
        a[at + TOP:, :] = below - change
        a[at + TOP:, at:at + TOP] = w
    solved = a[ranks:, :]
    first[me_c] = jnp.sum(solved * solved, axis=0, keepdims=True)
    for buf, me, n_all, ss, sr, name in (
        (first, me_c, nc, qs, qr, "col"), (second, me_r, nr, us, ur, "row")
    ):
        if name == "row":
            total = first[0]
            for n in range(1, nc):
                total = total + first[n]
            second[me_r] = total
        slot = buf.at[me]
        copies += [
            push(slot, slot, ss.at[n], sr.at[n], {name: lax.rem(me + n, n_all)}) for n in range(1, n_all)
        ]
        for copy in copies[1 - n_all:]:
            copy.start()
        if name == "col":
            solved_ref[...] = solved
        for n in range(1, n_all):
            came = buf.at[lax.rem(me + n_all - n, n_all)]
            push(slot, came, ss.at[n], sr.at[n], {name: lax.rem(me + n, n_all)}).wait_recv()
    total = second[0]
    for n in range(1, nr):
        total = total + second[n]
    squares_ref[...] = total
    for copy in copies + gcopies + ccopies + rcopies:
        copy.wait_send()
    for n in range(1, nc):
        block_send(n).wait_send()


def local(tensor, factor_b, factor_c):
    depth, rows_i, cols_j = tensor.shape
    ranks = factor_c.shape[1]
    nr, nc = lax.axis_size("row"), lax.axis_size("col")
    share = rows_i // nc
    rows = ranks // (nr * nc)
    f32, bf16 = jnp.float32, jnp.bfloat16
    vmem = pl.BlockSpec(memory_space=pltpu.VMEM)
    hbm = pl.BlockSpec(memory_space=pl.ANY)
    dma = pltpu.SemaphoreType.DMA
    solved, squares = pl.pallas_call(
        functools.partial(whole_kernel, nr, nc),
        out_shape=(jax.ShapeDtypeStruct((share, ranks), f32), jax.ShapeDtypeStruct((1, ranks), f32)),
        in_specs=[hbm, hbm, hbm],
        out_specs=(vmem, vmem),
        scratch_shapes=[
            pltpu.VMEM((ranks, cols_j), f32),
            pltpu.VMEM((ranks, 3 * cols_j), bf16),
            pltpu.VMEM((ranks, ranks), f32),
            pltpu.VMEM((nc, rows, ranks), f32),
            pltpu.VMEM((nc, rows, ranks), f32),
            pltpu.VMEM((nr, nc, rows, ranks), f32),
            pltpu.VMEM((nc, share, ranks), f32),
            pltpu.VMEM((nc, share, ranks), f32),
            pltpu.VMEM((nc, depth, share, cols_j), f32),
            pltpu.VMEM((depth, ranks), f32),
            pltpu.VMEM((ranks + share, ranks), f32),
            pltpu.VMEM((nc, 1, ranks), f32),
            pltpu.VMEM((nr, 1, ranks), f32),
            dma((nc,)), dma((2,)), dma((nr,)), dma((nr,)), dma((nc,)), dma((nc,)), dma((nc,)), dma((nc,)),
            dma((nr,)), dma((nr,)), dma((nc,)), dma((nc,)), dma((nc,)), dma((nc,)), dma((nr,)), dma((nr,)),
        ],
        compiler_params=pltpu.CompilerParams(
            collective_id=0, has_side_effects=True, vmem_limit_bytes=40 * 2**20
        ),
        name="whole",
    )(tensor, factor_b.T, factor_c)
    col_scale = jnp.sqrt(squares / (rows_i * nr) + eps)
    return (solved / col_scale, col_scale.reshape(ranks))


def solution(mesh):
    return jax.shard_map(
        local,
        mesh=mesh,
        in_specs=(P(None, "row", "col"), P("col", "row"), P()),
        out_specs=(P(("row", "col"), None), P()),
        check_vma=False,
    )
```

time: 58 us -> 48.4 us (0.83)
  Pallas kernels: 48.1 us -> 41.8 us
  local copies, waits for them, and re-layouts: 8.84 us -> 4.98 us
  other arithmetic: 0 us -> 0.63 us
    pallas_call x3 -> x1, Pallas kernels: 48.1 us -> 41.8 us  [local(): pl.pallas_call(functools.partial(whole_kernel, nr, nc), out_shape=(jax.Sh...]
    unnamed x11 -> x8, local copies, waits for them, and re-layouts: 8.84 us -> 4.98 us
    div x0 -> x1, other arithmetic: none -> 0.63 us  [local(): return (solved / col_scale, col_scale.reshape(ranks))]
where the time goes in v2:
time: 48.4 us; the launch traced here: 48.1 us
  Pallas kernels  41.8 us (86%)
  local copies, waits for them, and re-layouts  4.98 us (10%)
  between operations  0.66 us (1%)
  other arithmetic  0.63 us (1%)
    pallas_call x1, Pallas kernels, local(): pl.pallas_call(functools.partial(whole_kernel, nr, nc), out_shape=(jax.Sh...  41.8 us
    unnamed x8, local copies, waits for them, and re-layouts  4.98 us

profile of v2, /device:TPU:0, one launch (start us, length us, event | category | flops | bytes accessed | tf_op | source)
XLA Modules:
  0.0 48.1 jit_solution(14613377687617311888)
XLA Ops:
  0.6 0.0 copy-start
  0.6 3.4 %copy-done = f32[32,256,256]{2,1,0:T(8,128)S(1)} copy-done((f32[32,256,256]{2,1,0:T(8,128)S(1)}, f32[32,256,256]{2,1,0:T(8,128)}, u32[]{:S(2)}) %copy-start) | copy-done | bytes 8388632
  4.0 0.0 copy-start.1
  4.0 0.8 %copy-done.1 = f32[256,64]{0,1:T(8,128)S(1)} copy-done((f32[256,64]{0,1:T(8,128)S(1)}, f32[256,64]{0,1:T(8,128)}, u32[]{:S(2)}) %copy-start.1) | copy-done | bytes 65560
  4.9 0.0 copy-start.2
  4.9 0.8 %copy-done.2 = f32[32,256]{1,0:T(8,128)S(1)} copy-done((f32[32,256]{1,0:T(8,128)S(1)}, f32[32,256]{1,0:T(8,128)}, u32[]{:S(2)}) %copy-start.2) | copy-done | bytes 32792
  5.6 41.8 %whole.1 = (f32[32,256]{1,0:T(8,128)S(1)}, f32[1,256]{1,0:T(1,128)S(1)}) custom-call(f32[32,256,256]{2,1,0:T(8,128)S(1)} %copy-done, f32[64,256]{1,0:T(8,128)S(1)} %bitcast.2, f32[32,256]{1,0:T(8,128)S(1)} %copy-done.2), custom_call_target="tpu_custom_call" | custom-call | tf_op jit(solution)/shard_map/whole/pallas_call | solution.py:243
  47.5 0.0 copy-start.3
  47.5 0.6 %broadcast_divide_fusion = f32[32,256]{1,0:T(8,128)} fusion(f32[32,256]{1,0:T(8,128)S(1)} %get-tuple-element.4, f32[256]{0:T(256)S(1)} %bitcast.3), kind=kLoop, calls=%fused_computation | loop fusion | flops 8192 | bytes 66560 | tf_op jit(solution)/shard_map/div | solution.py:271
  48.1 0.0 copy-done.3
  (1 shorter events, 0.0 us)
Async XLA Ops:
  0.6 3.4 %copy-start = (f32[32,256,256]{2,1,0:T(8,128)S(1)}, f32[32,256,256]{2,1,0:T(8,128)}, u32[]{:S(2)}) copy-start(f32[32,256,256]{2,1,0:T(8,128)} %t_ref.1) | copy-start | bytes 25165828
  4.0 0.8 %copy-start.1 = (f32[256,64]{0,1:T(8,128)S(1)}, f32[256,64]{0,1:T(8,128)}, u32[]{:S(2)}) copy-start(f32[256,64]{0,1:T(8,128)} %param.4) | copy-start | bytes 196612
  4.9 0.8 %copy-start.2 = (f32[32,256]{1,0:T(8,128)S(1)}, f32[32,256]{1,0:T(8,128)}, u32[]{:S(2)}) copy-start(f32[32,256]{1,0:T(8,128)} %c_hbm.1) | copy-start | bytes 98308
  47.5 0.6 %copy-start.3 = (f32[1,256]{1,0:T(1,128)}, f32[1,256]{1,0:T(1,128)S(1)}, u32[]{:S(2)}) copy-start(f32[1,256]{1,0:T(1,128)S(1)} %add_sqrt_fusion) | copy-start | bytes 3076

commit v3 on v2

--- a/solution.py
+++ b/solution.py
@@ -35,6 +35,10 @@
     return lax.dot_general(
         a, b, (((1,), (1,)), ((), ())), precision=precision, preferred_element_type=jnp.float32
     )
+
+
+def line(held, p):
+    return jnp.broadcast_to(held[p:p + 1], held.shape)
 
 
 def invert_block(tile, low):
@@ -54,16 +58,26 @@
             [jnp.broadcast_to(v[i][:, base + s * SUB + j:base + s * SUB + j + 1], wide) for j in range(SUB)]
             for i in range(size)
         ]
-        head, c = v[s], cols[s]
-        for p in range(SUB):
-            inv = 1.0 / jnp.broadcast_to(c[p][p:p + 1], wide)
-            here = row == p
-            pivot = jnp.broadcast_to(head[p:p + 1], wide) * inv
-            head = jnp.where(here, pivot, head - c[p] * pivot)
-            for j in range(p + 1, SUB):
-                q = jnp.broadcast_to(c[j][p:p + 1], wide) * inv
-                c[j] = jnp.where(here, q, c[j] - c[p] * q)
-        lines = [jnp.broadcast_to(head[j:j + 1], wide) for j in range(SUB)]
+        head, c = v[s], list(cols[s])
+        for p in range(0, SUB, 2):
+            cp, cq = c[p], c[p + 1]
+            first, second = row == p, row == p + 1
+            here = first | second
+            a, d = line(cp, p), line(cq, p + 1)
+            b, e = line(cq, p), line(cp, p + 1)
+            inv = 1.0 / (a * d - b * e)
+            cp = jnp.where(first, -1.0, jnp.where(second, 0.0, cp))
+            cq = jnp.where(second, -1.0, jnp.where(first, 0.0, cq))
+
+            def step(held):
+                x, y = line(held, p), line(held, p + 1)
+                change = cp * (d * x - b * y) + cq * (a * y - e * x)
+                return jnp.where(here, 0.0, held) - change * inv
+
+            for j in range(p + 2, SUB):
+                c[j] = step(c[j])
+            head = step(head)
+        lines = [line(head, j) for j in range(SUB)]
         for i in range(size):
             if i == s:
                 v[i] = head
@@ -126,9 +140,10 @@
         p = lax.rem(me_c + n, nc)
         gcopies.append(push(gsend.at[p], grecv.at[n], gs.at[n], gr_.at[n], {"col": p}))
         gcopies[-1].start()
-    hi = full.astype(jnp.bfloat16)
-    lo = (full - hi.astype(jnp.float32)).astype(jnp.bfloat16)
-    bcat[...] = jnp.concatenate([hi, hi, lo], axis=1)
+    turned = full.T
+    hi = turned.astype(jnp.bfloat16)
+    lo = (turned - hi.astype(jnp.float32)).astype(jnp.bfloat16)
+    bcat[...] = jnp.concatenate([hi, hi, lo], axis=0)
 
     group = max(1, 512 // share)
 
@@ -139,7 +154,9 @@
             slab = tbuf[n, g:g + group].reshape(group * share, tbuf.shape[3])
             th = slab.astype(jnp.bfloat16)
             tl = (slab - th.astype(jnp.float32)).astype(jnp.bfloat16)
-            product = nt_dot(jnp.concatenate([th, tl, th], axis=1), bcat[...])
+            product = jnp.dot(
+                jnp.concatenate([th, tl, th], axis=1), bcat[...], preferred_element_type=jnp.float32
+            )
             for f in range(group):
                 total += product[f * share:(f + 1) * share] * c_ref[g + f:g + f + 1, :]
         msend[n] = total
@@ -180,25 +197,44 @@
     for n in range(1, nr):
         came = gfull.at[lax.rem(me_r + nr - n, nr)]
         push(gfull.at[me_r], came, rs.at[n], rr.at[n], {"row": lax.rem(me_r + n, nr)}).wait_recv()
+    lanes = lax.broadcasted_iota(jnp.int32, (rows, ranks), 1)
+    subs = lax.broadcasted_iota(jnp.int32, (rows, ranks), 0)
+    diagonal = jnp.zeros((rows, ranks), jnp.float32)
     for r in range(nr):
         for k in range(nc):
             at = (r * nc + k) * rows
-            a[at:at + rows, :] = gfull[r, k] * gc[at:at + rows, :]
-
-    for b in range(ranks // TOP):
+            held = gfull[r, k] * gc[at:at + rows, :]
+            a[at:at + rows, :] = held
+            diagonal = jnp.where(lanes == subs + at, held, diagonal)
+    unit = 1.0 / jnp.sum(diagonal, axis=0, keepdims=True)
+    a[0:ranks, :] = a[0:ranks, :] * unit
+
+    def inverted(b):
         at = b * TOP
-        inverse = invert_block(a[at:at + TOP, (b // 2) * 2 * TOP:(b // 2 + 1) * 2 * TOP], b % 2 == 0)
-        if b == 0:
-            total = msend[0]
-            for n in range(1, nc):
-                block_send(n).wait_recv()
-                total = total + mrecv[n]
-            a[ranks:, :] = total
-        below = a[at + TOP:, :]
-        w = jnp.dot(below[:, at:at + TOP], inverse, precision=HIGH, preferred_element_type=jnp.float32)
+        return invert_block(a[at:at + TOP, (b // 2) * 2 * TOP:(b // 2 + 1) * 2 * TOP], b % 2 == 0)
+
+    def update(low, high, at, inverse):
+        held = a[low:high, :]
+        w = jnp.dot(held[:, at:at + TOP], inverse, precision=HIGH, preferred_element_type=jnp.float32)
         change = jnp.dot(w, a[at:at + TOP, :], precision=HIGH, preferred_element_type=jnp.float32)
-        a[at + TOP:, :] = below - change
-        a[at + TOP:, at:at + TOP] = w
+        a[low:high, :] = held - change
+        a[low:high, at:at + TOP] = w
+
+    inverse = inverted(0)
+    total = msend[0]
+    for n in range(1, nc):
+        block_send(n).wait_recv()
+        total = total + mrecv[n]
+    a[ranks:, :] = total * unit
+    for at in range(0, ranks, TOP):
+        low, high = at + TOP, a.shape[0]
+        if low < ranks:
+            update(low, low + TOP, at, inverse)
+            later = inverted(low // TOP)
+            update(low + TOP, high, at, inverse)
+            inverse = later
+        else:
+            update(low, high, at, inverse)
     solved = a[ranks:, :]
     first[me_c] = jnp.sum(solved * solved, axis=0, keepdims=True)
     for buf, me, n_all, ss, sr, name in (
@@ -238,7 +274,7 @@
     rows = ranks // (nr * nc)
     f32, bf16 = jnp.float32, jnp.bfloat16
     vmem = pl.BlockSpec(memory_space=pltpu.VMEM)
-    hbm = pl.BlockSpec(memory_space=pl.ANY)
+    hbm = pl.BlockSpec(memory_space=pltpu.HBM)
     dma = pltpu.SemaphoreType.DMA
     solved, squares = pl.pallas_call(
         functools.partial(whole_kernel, nr, nc),
@@ -247,7 +283,7 @@
         out_specs=(vmem, vmem),
         scratch_shapes=[
             pltpu.VMEM((ranks, cols_j), f32),
-            pltpu.VMEM((ranks, 3 * cols_j), bf16),
+            pltpu.VMEM((3 * cols_j, ranks), bf16),
             pltpu.VMEM((ranks, ranks), f32),
             pltpu.VMEM((nc, rows, ranks), f32),
             pltpu.VMEM((nc, rows, ranks), f32),

time: 48.4 us -> 47.4 us (0.979)
  Pallas kernels: 41.8 us -> 40.9 us
    pallas_call x1, Pallas kernels: 41.8 us -> 40.9 us  [local(): pl.pallas_call(functools.partial(whole_kernel, nr, nc), out_shape=(jax.Sh...]
where the time goes in v3:
time: 47.4 us; the launch traced here: 47.2 us
  Pallas kernels  40.9 us (86%)
  local copies, waits for them, and re-layouts  4.98 us (11%)
  between operations  0.66 us (1%)
  other arithmetic  0.63 us (1%)
    pallas_call x1, Pallas kernels, local(): pl.pallas_call(functools.partial(whole_kernel, nr, nc), out_shape=(jax.Sh...  40.9 us
    unnamed x8, local copies, waits for them, and re-layouts  4.98 us

profile of v3, /device:TPU:0, one launch (start us, length us, event | category | flops | bytes accessed | tf_op | source)
XLA Modules:
  0.0 47.2 jit_solution(2986938414635962225)
XLA Ops:
  0.6 0.0 copy-start
  0.6 3.4 %copy-done = f32[32,256,256]{2,1,0:T(8,128)S(1)} copy-done((f32[32,256,256]{2,1,0:T(8,128)S(1)}, f32[32,256,256]{2,1,0:T(8,128)}, u32[]{:S(2)}) %copy-start) | copy-done | bytes 8388632
  4.0 0.0 copy-start.1
  4.0 0.8 %copy-done.1 = f32[256,64]{0,1:T(8,128)S(1)} copy-done((f32[256,64]{0,1:T(8,128)S(1)}, f32[256,64]{0,1:T(8,128)}, u32[]{:S(2)}) %copy-start.1) | copy-done | bytes 65560
  4.9 0.0 copy-start.2
  4.9 0.8 %copy-done.2 = f32[32,256]{1,0:T(8,128)S(1)} copy-done((f32[32,256]{1,0:T(8,128)S(1)}, f32[32,256]{1,0:T(8,128)}, u32[]{:S(2)}) %copy-start.2) | copy-done | bytes 32792
  5.6 40.9 %whole.1 = (f32[32,256]{1,0:T(8,128)S(1)}, f32[1,256]{1,0:T(1,128)S(1)}) custom-call(f32[32,256,256]{2,1,0:T(8,128)S(1)} %copy-done, f32[64,256]{1,0:T(8,128)S(1)} %bitcast.2, f32[32,256]{1,0:T(8,128)S(1)} %copy-done.2), custom_call_target="tpu_custom_call" | custom-call | tf_op jit(solution)/shard_map/whole/pallas_call | solution.py:279
  46.5 0.0 copy-start.3
  46.5 0.6 %broadcast_divide_fusion = f32[32,256]{1,0:T(8,128)} fusion(f32[32,256]{1,0:T(8,128)S(1)} %get-tuple-element.4, f32[256]{0:T(256)S(1)} %bitcast.3), kind=kLoop, calls=%fused_computation | loop fusion | flops 8192 | bytes 66560 | tf_op jit(solution)/shard_map/div | solution.py:307
  47.2 0.0 copy-done.3
  (1 shorter events, 0.0 us)
Async XLA Ops:
  0.6 3.4 %copy-start = (f32[32,256,256]{2,1,0:T(8,128)S(1)}, f32[32,256,256]{2,1,0:T(8,128)}, u32[]{:S(2)}) copy-start(f32[32,256,256]{2,1,0:T(8,128)} %t_ref.1) | copy-start | bytes 25165828
  4.0 0.8 %copy-start.1 = (f32[256,64]{0,1:T(8,128)S(1)}, f32[256,64]{0,1:T(8,128)}, u32[]{:S(2)}) copy-start(f32[256,64]{0,1:T(8,128)} %param.4) | copy-start | bytes 196612
  4.9 0.8 %copy-start.2 = (f32[32,256]{1,0:T(8,128)S(1)}, f32[32,256]{1,0:T(8,128)}, u32[]{:S(2)}) copy-start(f32[32,256]{1,0:T(8,128)} %c_hbm.1) | copy-start | bytes 98308
  46.5 0.6 %copy-start.3 = (f32[1,256]{1,0:T(1,128)}, f32[1,256]{1,0:T(1,128)S(1)}, u32[]{:S(2)}) copy-start(f32[1,256]{1,0:T(1,128)S(1)} %add_sqrt_fusion) | copy-start | bytes 3076

commit v4 on v3

--- a/solution.py
+++ b/solution.py
@@ -65,7 +65,7 @@
             here = first | second
             a, d = line(cp, p), line(cq, p + 1)
             b, e = line(cq, p), line(cp, p + 1)
-            inv = 1.0 / (a * d - b * e)
+            inv = pl.reciprocal(a * d - b * e, approx=True)
             cp = jnp.where(first, -1.0, jnp.where(second, 0.0, cp))
             cq = jnp.where(second, -1.0, jnp.where(first, 0.0, cq))
 
@@ -92,8 +92,8 @@
 
 def whole_kernel(
     nr, nc, t_ref, b_hbm, c_hbm, solved_ref, squares_ref,
-    bt, bcat, gc, gsend, grecv, gfull, msend, mrecv, tbuf, c_ref, a, first, second,
-    tsem, lsem, bs, br, gs, gr_, cs, cr, rs, rr, ms, mr, qs, qr, us, ur,
+    bt, bcat, gc, gsend, grecv, gfull, msend, mrecv, tbuf, tcat, c_ref, a, parts,
+    tsem, lsem, bs, br, gs, gr_, cs, cr, rs, rr, ms, mr, qs, qr,
 ):
     me_r, me_c = lax.axis_index("row"), lax.axis_index("col")
     depth, share = tbuf.shape[1], tbuf.shape[2]
@@ -125,6 +125,19 @@
     gc[...] = lax.dot_general(
         c, c, (((0,), (0,)), ((), ())), precision=HIGH, preferred_element_type=jnp.float32
     )
+    group = max(1, 512 // share)
+    wide = tbuf.shape[3]
+
+    @pl.loop(1, nc + 1)
+    def _(step):
+        n = lax.rem(step, nc)
+        load(n).wait()
+        for g in range(0, depth, group):
+            slab = tbuf[n, g:g + group].reshape(group * share, wide)
+            th = slab.astype(jnp.bfloat16)
+            tcat[n, g * share:(g + group) * share, :wide] = th
+            tcat[n, g * share:(g + group) * share, wide:] = (slab - th.astype(jnp.float32)).astype(jnp.bfloat16)
+
     for n in range(1, nr):
         came = pl.ds(pl.multiple_of(lax.rem(me_r + nr - n, nr) * rb, rb), rb)
         push(b_hbm, bt.at[came], bs.at[n], br.at[n], {"row": lax.rem(me_r + n, nr)}).wait_recv()
@@ -145,17 +158,12 @@
     lo = (turned - hi.astype(jnp.float32)).astype(jnp.bfloat16)
     bcat[...] = jnp.concatenate([hi, hi, lo], axis=0)
 
-    group = max(1, 512 // share)
-
     def block(n):
-        load(n).wait()
         total = jnp.zeros((share, ranks), jnp.float32)
         for g in range(0, depth, group):
-            slab = tbuf[n, g:g + group].reshape(group * share, tbuf.shape[3])
-            th = slab.astype(jnp.bfloat16)
-            tl = (slab - th.astype(jnp.float32)).astype(jnp.bfloat16)
+            halves = tcat[n, g * share:(g + group) * share, :]
             product = jnp.dot(
-                jnp.concatenate([th, tl, th], axis=1), bcat[...], preferred_element_type=jnp.float32
+                jnp.concatenate([halves, halves[:, :wide]], axis=1), bcat[...], preferred_element_type=jnp.float32
             )
             for f in range(group):
                 total += product[f * share:(f + 1) * share] * c_ref[g + f:g + f + 1, :]
@@ -236,34 +244,29 @@
         else:
             update(low, high, at, inverse)
     solved = a[ranks:, :]
-    first[me_c] = jnp.sum(solved * solved, axis=0, keepdims=True)
-    for buf, me, n_all, ss, sr, name in (
-        (first, me_c, nc, qs, qr, "col"), (second, me_r, nr, us, ur, "row")
-    ):
-        if name == "row":
-            total = first[0]
-            for n in range(1, nc):
-                total = total + first[n]
-            second[me_r] = total
-        slot = buf.at[me]
-        copies += [
-            push(slot, slot, ss.at[n], sr.at[n], {name: lax.rem(me + n, n_all)}) for n in range(1, n_all)
-        ]
-        for copy in copies[1 - n_all:]:
-            copy.start()
-        if name == "col":
-            solved_ref[...] = solved
-        for n in range(1, n_all):
-            came = buf.at[lax.rem(me + n_all - n, n_all)]
-            push(slot, came, ss.at[n], sr.at[n], {name: lax.rem(me + n, n_all)}).wait_recv()
-    total = second[0]
-    for n in range(1, nr):
-        total = total + second[n]
+    parts[me_r, me_c] = jnp.sum(solved * solved, axis=0, keepdims=True)
+
+    def part_send(i, k):
+        slot = parts.at[me_r, me_c]
+        device = {"row": lax.rem(me_r + i, nr), "col": lax.rem(me_c + k, nc)}
+        return push(slot, slot, qs.at[i, k], qr.at[i, k], device)
+
+    others = [(i, k) for i in range(nr) for k in range(nc) if i or k]
+    for i, k in others:
+        part_send(i, k).start()
+    solved_ref[...] = solved
+    for i, k in others:
+        came = parts.at[lax.rem(me_r + nr - i, nr), lax.rem(me_c + nc - k, nc)]
+        device = {"row": lax.rem(me_r + i, nr), "col": lax.rem(me_c + k, nc)}
+        push(parts.at[me_r, me_c], came, qs.at[i, k], qr.at[i, k], device).wait_recv()
+    total = jnp.sum(parts[...].reshape(nr * nc, 1, ranks), axis=0)
     squares_ref[...] = total
     for copy in copies + gcopies + ccopies + rcopies:
         copy.wait_send()
     for n in range(1, nc):
         block_send(n).wait_send()
+    for i, k in others:
+        part_send(i, k).wait_send()
 
 
 def local(tensor, factor_b, factor_c):
@@ -291,15 +294,15 @@
             pltpu.VMEM((nc, share, ranks), f32),
             pltpu.VMEM((nc, share, ranks), f32),
             pltpu.VMEM((nc, depth, share, cols_j), f32),
+            pltpu.VMEM((nc, depth * share, 2 * cols_j), bf16),
             pltpu.VMEM((depth, ranks), f32),
             pltpu.VMEM((ranks + share, ranks), f32),
-            pltpu.VMEM((nc, 1, ranks), f32),
-            pltpu.VMEM((nr, 1, ranks), f32),
+            pltpu.VMEM((nr, nc, 1, ranks), f32),
             dma((nc,)), dma((2,)), dma((nr,)), dma((nr,)), dma((nc,)), dma((nc,)), dma((nc,)), dma((nc,)),
-            dma((nr,)), dma((nr,)), dma((nc,)), dma((nc,)), dma((nc,)), dma((nc,)), dma((nr,)), dma((nr,)),
+            dma((nr,)), dma((nr,)), dma((nc,)), dma((nc,)), dma((nr, nc)), dma((nr, nc)),
         ],
         compiler_params=pltpu.CompilerParams(
-            collective_id=0, has_side_effects=True, vmem_limit_bytes=40 * 2**20
+            collective_id=0, has_side_effects=True, vmem_limit_bytes=62 * 2**20
         ),
         name="whole",
     )(tensor, factor_b.T, factor_c)

time: 47.4 us -> 42.9 us (0.905)
  local copies, waits for them, and re-layouts: 4.98 us -> 0.01 us
  other arithmetic: 0.63 us -> 2.03 us
  Pallas kernels: 40.9 us -> 40 us
    unnamed x8 -> x2, local copies, waits for them, and re-layouts: 4.98 us -> 0.01 us
    pallas_call x1, Pallas kernels: 40.9 us -> 40 us  [local(): pl.pallas_call(functools.partial(whole_kernel, nr, nc), out_shape=(jax.Sh...]
    div x1, other arithmetic: 0.63 us -> 1.39 us  [local(): return (solved / col_scale, col_scale.reshape(ranks))]
    sqrt x1, other arithmetic: 0.01 us -> 0.64 us  [local(): col_scale = jnp.sqrt(squares / (rows_i * nr) + eps)]
where the time goes in v4:
time: 42.9 us; the launch traced here: 42.7 us
  Pallas kernels  40 us (93%)
  other arithmetic  2.03 us (5%)
  between operations  0.64 us (1%)
    pallas_call x1, Pallas kernels, local(): pl.pallas_call(functools.partial(whole_kernel, nr, nc), out_shape=(jax.Sh...  40 us
    div x1, other arithmetic, local(): return (solved / col_scale, col_scale.reshape(ranks))  1.39 us

profile of v4, /device:TPU:0, one launch (start us, length us, event | category | flops | bytes accessed | tf_op | source)
XLA Modules:
  0.0 42.7 jit_solution(13180855698776110587)
XLA Ops:
  0.6 40.0 %whole.1 = (f32[32,256]{1,0:T(8,128)}, f32[1,256]{1,0:T(1,128)}) custom-call(f32[32,256,256]{2,1,0:T(8,128)} %t_ref.1, f32[64,256]{1,0:T(8,128)} %bitcast.2, f32[32,256]{1,0:T(8,128)} %c_hbm.1), custom_call_target="tpu_custom_call" | custom-call | tf_op jit(solution)/shard_map/whole/pallas_call | solution.py:282
  40.6 0.6 %add_sqrt_fusion = f32[1,256]{1,0:T(1,128)S(1)} fusion(f32[1,256]{1,0:T(1,128)} %get-tuple-element.5), kind=kLoop, calls=%fused_computation.1 | loop fusion | flops 512 | bytes 2048 | tf_op jit(solution)/shard_map/sqrt | solution.py:309
  41.3 0.0 copy-start
  41.3 1.4 %broadcast_divide_fusion = f32[32,256]{1,0:T(8,128)} fusion(f32[32,256]{1,0:T(8,128)} %get-tuple-element.4, f32[256]{0:T(256)S(1)} %bitcast.3), kind=kLoop, calls=%fused_computation | loop fusion | flops 8192 | bytes 66560 | tf_op jit(solution)/shard_map/div | solution.py:310
  42.7 0.0 copy-done
Async XLA Ops:
  41.3 1.4 %copy-start = (f32[1,256]{1,0:T(1,128)}, f32[1,256]{1,0:T(1,128)S(1)}, u32[]{:S(2)}) copy-start(f32[1,256]{1,0:T(1,128)S(1)} %add_sqrt_fusion) | copy-start | bytes 3076

commit v5 on v4

--- a/solution.py
+++ b/solution.py
@@ -112,14 +112,52 @@
     c_copy = pltpu.make_async_copy(c_hbm, c_ref, lsem.at[1])
     own_copy.start()
     c_copy.start()
-    for n in list(range(1, nc)) + [0]:
+    early = nc // 4
+    for n in range(1, early + 1):
         load(n).start()
     greeted()
 
-    copies = []
-    for n in range(1, nr):
-        copies.append(push(b_hbm, bt.at[mine_rows], bs.at[n], br.at[n], {"row": lax.rem(me_r + n, nr)}))
-        copies[-1].start()
+    mate = me_r + 1 - 2 * lax.rem(me_r, 2)
+    hops = range(2, nr, 2)
+
+    def slab(n):
+        return lax.rem(me_r + nr - n, nr)
+
+    def passed(n):
+        return lax.rem(mate + nr - n, nr)
+
+    def row_copy(src, dst, ssems, rsems, n, r):
+        return push(src, dst, ssems.at[n], rsems.at[n], {"row": r})
+
+    def place(r):
+        return bt.at[pl.ds(pl.multiple_of(r * rb, rb), rb)]
+
+    def gram_place(r):
+        return gfull.at[r]
+
+    def spread(src, at, ssems, rsems):
+        made = [row_copy(src, at(me_r), ssems, rsems, n, lax.rem(me_r + n, nr)) for n in hops]
+        made.append(row_copy(src, at(me_r), ssems, rsems, 1, mate))
+        for copy in made:
+            copy.start()
+        return made
+
+    def hand_on(at, ssems, rsems):
+        made = []
+        for n in hops:
+            row_copy(at(slab(n)), at(slab(n)), ssems, rsems, n, lax.rem(me_r + n, nr)).wait_recv()
+            made.append(row_copy(at(slab(n)), at(slab(n)), ssems, rsems, n + 1, mate))
+            made[-1].start()
+        return made
+
+    def gathered(at, ssems, rsems):
+        row_copy(at(mate), at(mate), ssems, rsems, 1, mate).wait_recv()
+        for n in hops:
+            row_copy(at(passed(n)), at(passed(n)), ssems, rsems, n + 1, mate).wait_recv()
+
+    copies = spread(b_hbm, place, bs, br)
+    for n in list(range(early + 1, nc)) + [0]:
+        load(n).start()
     c_copy.wait()
     c = c_ref[...]
     gc[...] = lax.dot_general(
@@ -128,8 +166,7 @@
     group = max(1, 512 // share)
     wide = tbuf.shape[3]
 
-    @pl.loop(1, nc + 1)
-    def _(step):
+    def split(step):
         n = lax.rem(step, nc)
         load(n).wait()
         for g in range(0, depth, group):
@@ -138,9 +175,10 @@
             tcat[n, g * share:(g + group) * share, :wide] = th
             tcat[n, g * share:(g + group) * share, wide:] = (slab - th.astype(jnp.float32)).astype(jnp.bfloat16)
 
-    for n in range(1, nr):
-        came = pl.ds(pl.multiple_of(lax.rem(me_r + nr - n, nr) * rb, rb), rb)
-        push(b_hbm, bt.at[came], bs.at[n], br.at[n], {"row": lax.rem(me_r + n, nr)}).wait_recv()
+    pl.loop(1, nc // 2 + 1)(split)
+    copies += hand_on(place, bs, br)
+    pl.loop(nc // 2 + 1, nc + 1)(split)
+    gathered(place, bs, br)
 
     own_copy.wait()
     full = bt[...]
@@ -178,33 +216,28 @@
             block(n)
             block_send(n).start()
 
-    cut1, cut2 = nc // 4 + 1, nc // 2 + 1
-    blocks(1, cut1)
+    cuts = [1 + nc * k // 4 for k in range(4)] + [nc]
+    blocks(cuts[0], cuts[1])
     for copy in gcopies:
         copy.wait_recv()
     total = gsend[me_c]
     for n in range(1, nc):
         total = total + grecv[n]
     gfull[me_r, me_c] = total
-    ccopies = []
     for n in range(1, nc):
         slot = gfull.at[me_r, me_c]
-        ccopies.append(push(slot, slot, cs.at[n], cr.at[n], {"col": lax.rem(me_c + n, nc)}))
-        ccopies[-1].start()
-    blocks(cut1, cut2)
+        copies.append(push(slot, slot, cs.at[n], cr.at[n], {"col": lax.rem(me_c + n, nc)}))
+        copies[-1].start()
+    blocks(cuts[1], cuts[2])
     for n in range(1, nc):
         came = gfull.at[me_r, lax.rem(me_c + nc - n, nc)]
         push(gfull.at[me_r, me_c], came, cs.at[n], cr.at[n], {"col": lax.rem(me_c + n, nc)}).wait_recv()
-    rcopies = []
-    for n in range(1, nr):
-        slot = gfull.at[me_r]
-        rcopies.append(push(slot, slot, rs.at[n], rr.at[n], {"row": lax.rem(me_r + n, nr)}))
-        rcopies[-1].start()
-    blocks(cut2, nc)
+    copies += spread(gfull.at[me_r], gram_place, rs, rr)
+    blocks(cuts[2], cuts[3])
+    copies += hand_on(gram_place, rs, rr)
+    blocks(cuts[3], cuts[4])
     block(0)
-    for n in range(1, nr):
-        came = gfull.at[lax.rem(me_r + nr - n, nr)]
-        push(gfull.at[me_r], came, rs.at[n], rr.at[n], {"row": lax.rem(me_r + n, nr)}).wait_recv()
+    gathered(gram_place, rs, rr)
     lanes = lax.broadcasted_iota(jnp.int32, (rows, ranks), 1)
     subs = lax.broadcasted_iota(jnp.int32, (rows, ranks), 0)
     diagonal = jnp.zeros((rows, ranks), jnp.float32)
@@ -261,7 +294,7 @@
         push(parts.at[me_r, me_c], came, qs.at[i, k], qr.at[i, k], device).wait_recv()
     total = jnp.sum(parts[...].reshape(nr * nc, 1, ranks), axis=0)
     squares_ref[...] = total
-    for copy in copies + gcopies + ccopies + rcopies:
+    for copy in copies + gcopies:
         copy.wait_send()
     for n in range(1, nc):
         block_send(n).wait_send()
@@ -302,7 +335,7 @@
             dma((nr,)), dma((nr,)), dma((nc,)), dma((nc,)), dma((nr, nc)), dma((nr, nc)),
         ],
         compiler_params=pltpu.CompilerParams(
-            collective_id=0, has_side_effects=True, vmem_limit_bytes=62 * 2**20
+            collective_id=0, has_side_effects=True, vmem_limit_bytes=56 * 2**20
         ),
         name="whole",
     )(tensor, factor_b.T, factor_c)

time: 42.9 us -> 45.6 us (1.063)
  Pallas kernels: 40 us -> 42.7 us
    pallas_call x1, Pallas kernels: 40 us -> 42.7 us  [local(): pl.pallas_call(functools.partial(whole_kernel, nr, nc), out_shape=(jax.Sh...]
where the time goes in v5:
time: 45.6 us; the launch traced here: 45.4 us
  Pallas kernels  42.7 us (94%)
  other arithmetic  2.03 us (4%)
  between operations  0.64 us (1%)
    pallas_call x1, Pallas kernels, local(): pl.pallas_call(functools.partial(whole_kernel, nr, nc), out_shape=(jax.Sh...  42.7 us
    div x1, other arithmetic, local(): return (solved / col_scale, col_scale.reshape(ranks))  1.39 us

profile of v5, /device:TPU:0, one launch (start us, length us, event | category | flops | bytes accessed | tf_op | source)
XLA Modules:
  0.0 45.4 jit_solution(7253125857561087346)
XLA Ops:
  0.6 42.7 %whole.1 = (f32[32,256]{1,0:T(8,128)}, f32[1,256]{1,0:T(1,128)}) custom-call(f32[32,256,256]{2,1,0:T(8,128)} %t_ref.1, f32[64,256]{1,0:T(8,128)} %bitcast.2, f32[32,256]{1,0:T(8,128)} %c_hbm.1), custom_call_target="tpu_custom_call" | custom-call | tf_op jit(solution)/shard_map/whole/pallas_call | solution.py:315
  43.4 0.6 %add_sqrt_fusion = f32[1,256]{1,0:T(1,128)S(1)} fusion(f32[1,256]{1,0:T(1,128)} %get-tuple-element.5), kind=kLoop, calls=%fused_computation.1 | loop fusion | flops 512 | bytes 2048 | tf_op jit(solution)/shard_map/sqrt | solution.py:342
  44.0 0.0 copy-start
  44.0 1.4 %broadcast_divide_fusion = f32[32,256]{1,0:T(8,128)} fusion(f32[32,256]{1,0:T(8,128)} %get-tuple-element.4, f32[256]{0:T(256)S(1)} %bitcast.3), kind=kLoop, calls=%fused_computation | loop fusion | flops 8192 | bytes 66560 | tf_op jit(solution)/shard_map/div | solution.py:343
  45.4 0.0 copy-done
Async XLA Ops:
  44.0 1.4 %copy-start = (f32[1,256]{1,0:T(1,128)}, f32[1,256]{1,0:T(1,128)S(1)}, u32[]{:S(2)}) copy-start(f32[1,256]{1,0:T(1,128)S(1)} %add_sqrt_fusion) | copy-start | bytes 3076

commit v6 on v4

--- a/solution.py
+++ b/solution.py
@@ -135,8 +135,8 @@
         for g in range(0, depth, group):
             slab = tbuf[n, g:g + group].reshape(group * share, wide)
             th = slab.astype(jnp.bfloat16)
-            tcat[n, g * share:(g + group) * share, :wide] = th
-            tcat[n, g * share:(g + group) * share, wide:] = (slab - th.astype(jnp.float32)).astype(jnp.bfloat16)
+            tcat[step - 1, g * share:(g + group) * share, :wide] = th
+            tcat[step - 1, g * share:(g + group) * share, wide:] = (slab - th.astype(jnp.float32)).astype(jnp.bfloat16)
 
     for n in range(1, nr):
         came = pl.ds(pl.multiple_of(lax.rem(me_r + nr - n, nr) * rb, rb), rb)
@@ -158,28 +158,33 @@
     lo = (turned - hi.astype(jnp.float32)).astype(jnp.bfloat16)
     bcat[...] = jnp.concatenate([hi, hi, lo], axis=0)
 
-    def block(n):
-        total = jnp.zeros((share, ranks), jnp.float32)
-        for g in range(0, depth, group):
-            halves = tcat[n, g * share:(g + group) * share, :]
-            product = jnp.dot(
-                jnp.concatenate([halves, halves[:, :wide]], axis=1), bcat[...], preferred_element_type=jnp.float32
-            )
-            for f in range(group):
-                total += product[f * share:(f + 1) * share] * c_ref[g + f:g + f + 1, :]
-        msend[n] = total
+    def pair(q):
+        halves = tcat[pl.ds(2 * q, 2)].reshape(2 * depth * share, 2 * wide)
+        product = jnp.dot(
+            jnp.concatenate([halves, halves[:, :wide]], axis=1), bcat[...], preferred_element_type=jnp.float32
+        )
+        for u in range(2):
+            total = jnp.zeros((share, ranks), jnp.float32)
+            for f in range(depth):
+                at = (u * depth + f) * share
+                total += product[at:at + share] * c_ref[f:f + 1, :]
+            msend[lax.rem(2 * q + u + 1, nc)] = total
 
     def block_send(n):
         return push(msend.at[n], mrecv.at[n], ms.at[n], mr.at[n], {"col": lax.rem(me_c + n, nc)})
 
-    def blocks(first, last):
+    def pairs(first, last):
         @pl.loop(first, last)
-        def _(n):
-            block(n)
-            block_send(n).start()
-
-    cut1, cut2 = nc // 4 + 1, nc // 2 + 1
-    blocks(1, cut1)
+        def _(q):
+            pair(q)
+            block_send(2 * q + 1).start()
+
+            @pl.when(2 * q + 2 < nc)
+            def _():
+                block_send(2 * q + 2).start()
+
+    cut1, cut2 = nc // 8, nc // 4
+    pairs(0, cut1)
     for copy in gcopies:
         copy.wait_recv()
     total = gsend[me_c]
@@ -191,7 +196,7 @@
         slot = gfull.at[me_r, me_c]
         ccopies.append(push(slot, slot, cs.at[n], cr.at[n], {"col": lax.rem(me_c + n, nc)}))
         ccopies[-1].start()
-    blocks(cut1, cut2)
+    pairs(cut1, cut2)
     for n in range(1, nc):
         came = gfull.at[me_r, lax.rem(me_c + nc - n, nc)]
         push(gfull.at[me_r, me_c], came, cs.at[n], cr.at[n], {"col": lax.rem(me_c + n, nc)}).wait_recv()
@@ -200,8 +205,7 @@
         slot = gfull.at[me_r]
         rcopies.append(push(slot, slot, rs.at[n], rr.at[n], {"row": lax.rem(me_r + n, nr)}))
         rcopies[-1].start()
-    blocks(cut2, nc)
-    block(0)
+    pairs(cut2, nc // 2)
     for n in range(1, nr):
         came = gfull.at[lax.rem(me_r + nr - n, nr)]
         push(gfull.at[me_r], came, rs.at[n], rr.at[n], {"row": lax.rem(me_r + n, nr)}).wait_recv()

time: 42.9 us -> 42.8 us (level)
  no operation moved by 1% of the time
where the time goes in v6:
time: 42.8 us; the launch traced here: 42.6 us
  Pallas kernels  39.9 us (93%)
  other arithmetic  2.03 us (5%)
  between operations  0.64 us (1%)
    pallas_call x1, Pallas kernels, local(): pl.pallas_call(functools.partial(whole_kernel, nr, nc), out_shape=(jax.Sh...  39.9 us
    div x1, other arithmetic, local(): return (solved / col_scale, col_scale.reshape(ranks))  1.39 us

profile of v6, /device:TPU:0, one launch (start us, length us, event | category | flops | bytes accessed | tf_op | source)
XLA Modules:
  0.0 42.6 jit_solution(12175364115419237633)
XLA Ops:
  0.6 39.9 %whole.1 = (f32[32,256]{1,0:T(8,128)}, f32[1,256]{1,0:T(1,128)}) custom-call(f32[32,256,256]{2,1,0:T(8,128)} %t_ref.1, f32[64,256]{1,0:T(8,128)} %bitcast.2, f32[32,256]{1,0:T(8,128)} %c_hbm.1), custom_call_target="tpu_custom_call" | custom-call | tf_op jit(solution)/shard_map/whole/pallas_call | solution.py:286
  40.6 0.6 %add_sqrt_fusion = f32[1,256]{1,0:T(1,128)S(1)} fusion(f32[1,256]{1,0:T(1,128)} %get-tuple-element.5), kind=kLoop, calls=%fused_computation.1 | loop fusion | flops 512 | bytes 2048 | tf_op jit(solution)/shard_map/sqrt | solution.py:313
  41.2 0.0 copy-start
  41.2 1.4 %broadcast_divide_fusion = f32[32,256]{1,0:T(8,128)} fusion(f32[32,256]{1,0:T(8,128)} %get-tuple-element.4, f32[256]{0:T(256)S(1)} %bitcast.3), kind=kLoop, calls=%fused_computation | loop fusion | flops 8192 | bytes 66560 | tf_op jit(solution)/shard_map/div | solution.py:314
  42.6 0.0 copy-done
Async XLA Ops:
  41.2 1.4 %copy-start = (f32[1,256]{1,0:T(1,128)}, f32[1,256]{1,0:T(1,128)S(1)}, u32[]{:S(2)}) copy-start(f32[1,256]{1,0:T(1,128)S(1)} %add_sqrt_fusion) | copy-start | bytes 3076

commit v7 on v6

--- a/solution.py
+++ b/solution.py
@@ -136,7 +136,8 @@
             slab = tbuf[n, g:g + group].reshape(group * share, wide)
             th = slab.astype(jnp.bfloat16)
             tcat[step - 1, g * share:(g + group) * share, :wide] = th
-            tcat[step - 1, g * share:(g + group) * share, wide:] = (slab - th.astype(jnp.float32)).astype(jnp.bfloat16)
+            tcat[step - 1, g * share:(g + group) * share, 2 * wide:] = th
+            tcat[step - 1, g * share:(g + group) * share, wide:2 * wide] = (slab - th.astype(jnp.float32)).astype(jnp.bfloat16)
 
     for n in range(1, nr):
         came = pl.ds(pl.multiple_of(lax.rem(me_r + nr - n, nr) * rb, rb), rb)
@@ -159,10 +160,8 @@
     bcat[...] = jnp.concatenate([hi, hi, lo], axis=0)
 
     def pair(q):
-        halves = tcat[pl.ds(2 * q, 2)].reshape(2 * depth * share, 2 * wide)
-        product = jnp.dot(
-            jnp.concatenate([halves, halves[:, :wide]], axis=1), bcat[...], preferred_element_type=jnp.float32
-        )
+        halves = tcat[pl.ds(2 * q, 2)].reshape(2 * depth * share, 3 * wide)
+        product = jnp.dot(halves, bcat[...], preferred_element_type=jnp.float32)
         for u in range(2):
             total = jnp.zeros((share, ranks), jnp.float32)
             for f in range(depth):
@@ -174,14 +173,11 @@
         return push(msend.at[n], mrecv.at[n], ms.at[n], mr.at[n], {"col": lax.rem(me_c + n, nc)})
 
     def pairs(first, last):
-        @pl.loop(first, last)
-        def _(q):
-            pair(q)
-            block_send(2 * q + 1).start()
-
-            @pl.when(2 * q + 2 < nc)
-            def _():
-                block_send(2 * q + 2).start()
+        pl.loop(first, last)(pair)
+
+    def send_pairs(first, last):
+        for n in range(2 * first + 1, min(2 * last + 1, nc)):
+            block_send(n).start()
 
     cut1, cut2 = nc // 8, nc // 4
     pairs(0, cut1)
@@ -196,6 +192,7 @@
         slot = gfull.at[me_r, me_c]
         ccopies.append(push(slot, slot, cs.at[n], cr.at[n], {"col": lax.rem(me_c + n, nc)}))
         ccopies[-1].start()
+    send_pairs(0, cut1)
     pairs(cut1, cut2)
     for n in range(1, nc):
         came = gfull.at[me_r, lax.rem(me_c + nc - n, nc)]
@@ -205,7 +202,12 @@
         slot = gfull.at[me_r]
         rcopies.append(push(slot, slot, rs.at[n], rr.at[n], {"row": lax.rem(me_r + n, nr)}))
         rcopies[-1].start()
-    pairs(cut2, nc // 2)
+    send_pairs(cut1, cut2)
+    middle = (cut2 + nc // 2) // 2
+    pairs(cut2, middle)
+    send_pairs(cut2, middle)
+    pairs(middle, nc // 2)
+    send_pairs(middle, nc // 2)
     for n in range(1, nr):
         came = gfull.at[lax.rem(me_r + nr - n, nr)]
         push(gfull.at[me_r], came, rs.at[n], rr.at[n], {"row": lax.rem(me_r + n, nr)}).wait_recv()
@@ -298,7 +300,7 @@
             pltpu.VMEM((nc, share, ranks), f32),
             pltpu.VMEM((nc, share, ranks), f32),
             pltpu.VMEM((nc, depth, share, cols_j), f32),
-            pltpu.VMEM((nc, depth * share, 2 * cols_j), bf16),
+            pltpu.VMEM((nc, depth * share, 3 * cols_j), bf16),
             pltpu.VMEM((depth, ranks), f32),
             pltpu.VMEM((ranks + share, ranks), f32),
             pltpu.VMEM((nr, nc, 1, ranks), f32),

time: 42.8 us -> 44.3 us (1.035)
  Pallas kernels: 39.9 us -> 41.4 us
    pallas_call x1, Pallas kernels: 39.9 us -> 41.4 us  [local(): pl.pallas_call(functools.partial(whole_kernel, nr, nc), out_shape=(jax.Sh...]
where the time goes in v7:
time: 44.3 us; the launch traced here: 44.1 us
  Pallas kernels  41.4 us (93%)
  other arithmetic  2.03 us (5%)
  between operations  0.64 us (1%)
    pallas_call x1, Pallas kernels, local(): pl.pallas_call(functools.partial(whole_kernel, nr, nc), out_shape=(jax.Sh...  41.4 us
    div x1, other arithmetic, local(): return (solved / col_scale, col_scale.reshape(ranks))  1.39 us

profile of v7, /device:TPU:0, one launch (start us, length us, event | category | flops | bytes accessed | tf_op | source)
XLA Modules:
  0.0 44.1 jit_solution(5890453957545455474)
XLA Ops:
  0.6 41.4 %whole.1 = (f32[32,256]{1,0:T(8,128)}, f32[1,256]{1,0:T(1,128)}) custom-call(f32[32,256,256]{2,1,0:T(8,128)} %t_ref.1, f32[64,256]{1,0:T(8,128)} %bitcast.2, f32[32,256]{1,0:T(8,128)} %c_hbm.1), custom_call_target="tpu_custom_call" | custom-call | tf_op jit(solution)/shard_map/whole/pallas_call | solution.py:288
  42.1 0.6 %add_sqrt_fusion = f32[1,256]{1,0:T(1,128)S(1)} fusion(f32[1,256]{1,0:T(1,128)} %get-tuple-element.5), kind=kLoop, calls=%fused_computation.1 | loop fusion | flops 512 | bytes 2048 | tf_op jit(solution)/shard_map/sqrt | solution.py:315
  42.7 0.0 copy-start
  42.7 1.4 %broadcast_divide_fusion = f32[32,256]{1,0:T(8,128)} fusion(f32[32,256]{1,0:T(8,128)} %get-tuple-element.4, f32[256]{0:T(256)S(1)} %bitcast.3), kind=kLoop, calls=%fused_computation | loop fusion | flops 8192 | bytes 66560 | tf_op jit(solution)/shard_map/div | solution.py:316
  44.1 0.0 copy-done
Async XLA Ops:
  42.7 1.4 %copy-start = (f32[1,256]{1,0:T(1,128)}, f32[1,256]{1,0:T(1,128)S(1)}, u32[]{:S(2)}) copy-start(f32[1,256]{1,0:T(1,128)S(1)} %add_sqrt_fusion) | copy-start | bytes 3076
